TPU v7x, 256 devices: a whole 4x4x8 slice. The times are simulated.
256 devices in a mesh: dp: 16 (over z, core), seq: 16 (over y, x).
Axes of the slice: x: 4, y: 4, z: 8, core: 2. Of those that a mesh axis runs over, the one named last changes fastest.
Arguments:
- loader_tokens: bfloat16 [16, 2048, 1408], P('dp', 'seq'), may hold values from -200 to 200
- destination: int32 [16, 2048], P('dp', 'seq'), may hold values from 0 to 32767, as said below
- segment_ids: int32 [16, 2048], P('dp'), may hold values from 0 to 7, as said below
- projection: bfloat16 [1408, 4224], replicated, may hold values from -3 to 3
Outputs:
- mixed_heads: bfloat16 [16, 2048, 1408], P('dp', 'seq')
Inputs may be any that keep to these rules, and one draw needn't show every extreme that they name: `destination`: every position of every pack receives exactly one token. A token's position lies in the same block of 128 positions as its own place in the loader's pack. The tokens of one loader pack in one such block go to a pack in numbers 0, 8 or 16, and 16 is reached in every block. `segment_ids`: sample numbers start at 0 in every pack and never fall along it. A sample is an image of 256 tokens or a clip of 512, 1024 or 2048 tokens, beginning at a multiple of its length. Some pack is one clip of 2048 tokens, and some pack holds only images.
All inputs are finite; a program needn't handle non-finite values.
Results may differ from a plain program's by a relative error of at most 0.008.
The roundings to bfloat16 on the way count: a program that leaves them out, or rounds other values in their place, can miss the bound.
Values may be sent and summed in bfloat16 or wider, within the bound.
A program may use at most 128 MiB of HBM per device.

v0:
```python
import jax
import jax.numpy as jnp
from jax import lax
from jax.sharding import PartitionSpec as P

HD = 88


MASKED_SCORE = -1e30
EPSILON = 1e-06


def normalize(rows):
    widened = rows.astype(jnp.float32)
    center = jnp.mean(widened, axis=-1, keepdims=True)
    spread = jnp.mean(jnp.square(widened - center), axis=-1, keepdims=True)
    return ((widened - center) * lax.rsqrt(spread + EPSILON)).astype(jnp.bfloat16)


def split_heads(block_data):
    return block_data.reshape(block_data.shape[0], -1, HD).transpose(1, 0, 2)


def update(carried, query_heads, query_seg, key_heads, value_heads, key_seg):
    peak, totals, accum = carried
    scores = jnp.einsum(
        "hqd,hkd->hqk", query_heads, key_heads, preferred_element_type=jnp.float32
    ) * HD ** (-0.5)
    allowed = (query_seg[:, None] == key_seg[None, :])[None]
    scores = jnp.where(allowed, scores, MASKED_SCORE)
    raised = jnp.maximum(peak, jnp.max(scores, axis=-1))
    weights = jnp.where(allowed, jnp.exp(scores - raised[..., None]), 0.0)
    factor = jnp.exp(peak - raised)
    totals = totals * factor + jnp.sum(weights, axis=-1)
    accum = accum * factor[..., None] + jnp.einsum(
        "hqk,hkd->hqd",
        weights.astype(jnp.bfloat16),
        value_heads,
        preferred_element_type=jnp.float32,
    )
    return (raised, totals, accum)


def visit_block(carried, query_heads, query_seg, key_heads, value_heads, key_seg):
    return update(carried, query_heads, query_seg, key_heads, value_heads, key_seg)


def empty_state(head_count, row_count):
    return (
        jnp.full((head_count, row_count), MASKED_SCORE, jnp.float32),
        jnp.zeros((head_count, row_count), jnp.float32),
        jnp.zeros((head_count, row_count, HD), jnp.float32),
    )


def per_device(loader_tokens, destination, segment_ids, projection):
    own_rows = loader_tokens[0]
    count_rows, model_width = own_rows.shape
    pack_count = lax.axis_size("dp")
    column = lax.axis_index("seq")
    pack_length = segment_ids.shape[1]
    capacity = 2 * count_rows // pack_count
    flat_target = destination[0]
    target = flat_target // pack_length
    position = flat_target % pack_length - column * count_rows
    member = (target[:, None] == jnp.arange(pack_count, dtype=jnp.int32)[None, :]).astype(jnp.int32)
    earlier = jnp.cumsum(member, axis=0) - member
    slot_rank = jnp.sum(earlier * member, axis=1)
    outgoing = (
        jnp.zeros((pack_count, capacity, model_width), jnp.bfloat16)
        .at[target, slot_rank]
        .set(own_rows)
    )
    out_slots = (
        jnp.full((pack_count, capacity), count_rows, jnp.int32).at[target, slot_rank].set(position)
    )
    arrived, arrived_slots = (
        lax.all_to_all(outgoing, "dp", split_axis=0, concat_axis=0, tiled=True),
        lax.all_to_all(out_slots, "dp", split_axis=0, concat_axis=0, tiled=True),
    )
    packed = (
        jnp.zeros((count_rows, model_width), jnp.bfloat16)
        .at[arrived_slots.reshape(-1)]
        .set(arrived.reshape(-1, model_width), mode="drop")
    )
    projected = jnp.dot(normalize(packed), projection, preferred_element_type=jnp.float32).astype(
        jnp.bfloat16
    )
    query_rows = projected[:, :model_width]
    key_rows = projected[:, model_width : 2 * model_width]
    value_rows = projected[:, 2 * model_width :]
    segment = segment_ids[0]
    own_seg = lax.dynamic_slice_in_dim(segment, column * count_rows, count_rows)
    head_queries = split_heads(query_rows)
    start_state = empty_state(head_queries.shape[0], count_rows)
    carried = start_state
    key_piece = lax.all_gather(key_rows, "seq", axis=0, tiled=True)
    value_piece = lax.all_gather(value_rows, "seq", axis=0, tiled=True)
    piece_rows = key_piece.shape[0]
    block_rows = 512

    def advance(inner, number):
        begin_row = number * block_rows
        key_block = split_heads(lax.dynamic_slice_in_dim(key_piece, begin_row, block_rows, 0))
        value_block = split_heads(lax.dynamic_slice_in_dim(value_piece, begin_row, block_rows, 0))
        key_seg = lax.dynamic_slice_in_dim(segment, begin_row, block_rows)
        return (visit_block(inner, head_queries, own_seg, key_block, value_block, key_seg), None)

    carried, unused = lax.scan(
        advance, carried, jnp.arange(piece_rows // block_rows, dtype=jnp.int32)
    )
    mixed = (
        (carried[2] / carried[1][..., None])
        .transpose(1, 0, 2)
        .reshape(count_rows, model_width)
        .astype(jnp.bfloat16)
    )
    return mixed[None]


def solution(mesh):
    placed = (P("dp", "seq", None), P("dp", "seq"), P("dp", None), P())
    return jax.shard_map(
        per_device, mesh=mesh, in_specs=placed, out_specs=P("dp", "seq", None), check_vma=False
    )
```

profile of v0, /device:TPU:1, one launch (start us, length us, event | category | flops | bytes accessed | tf_op | source)
XLA Modules:
  0.0 284.6 jit_solution(4337244745704440076)
XLA Ops:
  6.5 0.7 fusion.24
  7.3 0.2 reduce_window_sum.11
  7.5 0.2 select_reduce_fusion
  7.6 0.7 fusion.25
  8.3 0.6 broadcast_in_dim.56
  8.9 18.5 %scatter_fusion = s32[16,16]{1,0:T(8,128)} fusion(s32[16,16]{1,0:T(8,128)} %broadcast_in_dim.56, s32[128]{0:T(128)S(1)} %fusion.25, s32[128]{0:T(128)S(1)} %get-tuple-element.162), kind=kCustom, calls=%fused_computation | custom fusion | bytes 2560 | tf_op jit(solution)/shard_map/scatter | solution.py:75
  27.4 10.0 %all-to-all-start = ((s32[16,1,16]{2,1,0:T(1,128)}), s32[16,1,16]{2,1,0:T(1,128)S(1)}, u32[]{:S(2)}, u32[]{:S(2)}) async-start(s32[16,1,16]{2,1,0:T(1,128)} %bitcast.7), calls=%async_computation | async-start | bytes 16384 | tf_op jit(solution)/shard_map/all_to_all | solution.py:79
  37.4 0.9 broadcast_in_dim.57
  38.3 20.2 %scatter_fusion.1 = bf16[16,16,1408]{2,1,0:T(8,128)(2,1)} fusion(bf16[16,16,1408]{2,1,0:T(8,128)(2,1)} %broadcast_in_dim.57, s32[128]{0:T(128)S(1)} %fusion.25, bf16[128,1408]{1,0:T(8,128)(2,1)} %bitcast.98), kind=kCustom, calls=%fused_computation.1 | custom fusion | bytes 1082368 | tf_op jit(solution)/shard_map/scatter | solution.py:72
  58.5 7.3 %all-to-all-start.1 = ((bf16[16,16,1408]{2,1,0:T(8,128)(2,1)}), bf16[16,16,1408]{2,1,0:T(8,128)(2,1)S(1)}, u32[]{:S(2)}, u32[]{:S(2)}) async-start(bf16[16,16,1408]{2,1,0:T(8,128)(2,1)} %scatter_fusion.1), calls=%async_computation.1 | async-start | bytes 1441792 | tf_op jit(solution)/shard_map/all_to_all | solution.py:78
  65.9 0.5 broadcast.258
  66.4 0.7 reduce.3
  67.2 20.0 %all-to-all-done.1 = bf16[16,16,1408]{2,1,0:T(8,128)(2,1)S(1)} async-done(((bf16[16,16,1408]{2,1,0:T(8,128)(2,1)}), bf16[16,16,1408]{2,1,0:T(8,128)(2,1)S(1)}, u32[]{:S(2)}, u32[]{:S(2)}) %all-to-all-start.1) | async-done | bytes 720928 | tf_op jit(solution)/shard_map/all_to_all | solution.py:78
  87.2 1.8 scatter_custom_fusion.2
  89.1 0.2 fusion.15
  89.3 6.4 %convolution_convert_fusion = bf16[128,4224]{1,0:T(8,128)(2,1)S(1)} fusion(bf16[1408,4224]{1,0:T(8,128)(2,1)} %param.9, bf16[128,1408]{1,0:T(8,128)(2,1)S(1)} %scatter_custom_fusion.2, f32[128]{0:T(128)S(1)} %add_rsqrt_fusion, f32[128]{0:T(128)S(1)} %broadcast_multiply_fusion), kind=kOutput, calls=%fused_computation.22 | convolution fusion | flops 1523793920 | bytes 13337600 | tf_op jit(solution)/shard_map/dot_general | solution.py:86
  95.7 0.9 fusion.26
  96.7 0.7 all-gather.3.cloned.1.call-update
  97.4 0.7 dynamic-slice_bitcast_fusion
  98.1 0.2 copy.23
  98.3 59.2 %all-gather.5.cloned.1.call-done = bf16[2048,1408]{1,0:T(8,128)(2,1)} async-done(((bf16[128,1408]{1,0:T(8,128)(2,1)}), bf16[2048,1408]{1,0:T(8,128)(2,1)}) %all-gather.5.cloned.1.call-update) | async-done | bytes 5767184 | tf_op jit(solution)/shard_map/all_gather | solution.py:98
  157.6 66.1 %all-gather.3.cloned.1.call-done = bf16[2048,1408]{1,0:T(8,128)(2,1)} async-done(((bf16[128,1408]{1,0:T(8,128)(2,1)}), bf16[2048,1408]{1,0:T(8,128)(2,1)}) %all-gather.3.cloned.1.call-update) | async-done | bytes 5767184 | tf_op jit(solution)/shard_map/all_gather | solution.py:97
  223.6 52.0 %while.15 = (s32[]{:T(128)}, f32[16,128]{1,0:T(8,128)S(1)}, f32[16,128]{1,0:T(8,128)S(1)}, f32[16,128,88]{1,2,0:T(8,128)}, s32[128]{0:T(128)S(1)}, /*index=5*/s3...) while((s32[]{:T(128)}, f32[16,128]{1,0:T(8,128)S(1)}, ...), condition=%wide.region_10.11_spmd.clone, body=%wide.region_7.10_spmd.clone.sunk | while | flops 383346688 | bytes 40737580 | solution.py:109
  223.6 0.6 dynamic_slice.31
  224.9 0.8 dynamic_slice.32
  225.7 0.1 broadcast_compare_fusion.2
  225.8 3.1 %constant_dynamic-slice_fusion.3 = (bf16[512,1408]{1,0:T(8,128)(2,1)S(1)}, bf16[512,1408]{1,0:T(8,128)(2,1)}) fusion(bf16[2048,1408]{1,0:T(8,128)(2,1)} %get-tuple-element.274, s32[]{:T(128)S(6)} %select_n.132, bf16[2048,1408]{1,0:T(8,128)(2,1)} %get-tuple-element.272), kind=kLoop, calls=%fused_computation.17.clone.1 | loop fusion | bytes 5767172 | tf_op jit(solution)/shard_map/while/body/eval_jaxpr/dynamic_slice | solution.py:105
  228.9 1.7 copy.32
  230.6 1.6 copy.33
  232.2 1.0 fusion.43
  233.3 1.0 fusion.44
  234.3 1.4 fusion.46
  235.8 0.9 copy-done.2
  236.7 0.6 dynamic_slice.31
  237.9 0.8 dynamic_slice.32
  238.7 0.1 broadcast_compare_fusion.2
  238.8 3.1 %constant_dynamic-slice_fusion.3 = (bf16[512,1408]{1,0:T(8,128)(2,1)S(1)}, bf16[512,1408]{1,0:T(8,128)(2,1)}) fusion(bf16[2048,1408]{1,0:T(8,128)(2,1)} %get-tuple-element.274, s32[]{:T(128)S(6)} %select_n.132, bf16[2048,1408]{1,0:T(8,128)(2,1)} %get-tuple-element.272), kind=kLoop, calls=%fused_computation.17.clone.1 | loop fusion | bytes 5767172 | tf_op jit(solution)/shard_map/while/body/eval_jaxpr/dynamic_slice | solution.py:105
  242.0 1.7 copy.32
  243.6 1.6 copy.33
  245.3 1.0 fusion.43
  246.3 1.0 fusion.44
  247.3 1.4 fusion.46
  248.8 0.9 copy-done.2
  249.7 0.6 dynamic_slice.31
  250.9 0.8 dynamic_slice.32
  251.8 3.1 %constant_dynamic-slice_fusion.3 = (bf16[512,1408]{1,0:T(8,128)(2,1)S(1)}, bf16[512,1408]{1,0:T(8,128)(2,1)}) fusion(bf16[2048,1408]{1,0:T(8,128)(2,1)} %get-tuple-element.274, s32[]{:T(128)S(6)} %select_n.132, bf16[2048,1408]{1,0:T(8,128)(2,1)} %get-tuple-element.272), kind=kLoop, calls=%fused_computation.17.clone.1 | loop fusion | bytes 5767172 | tf_op jit(solution)/shard_map/while/body/eval_jaxpr/dynamic_slice | solution.py:105
  255.0 1.7 copy.32
  256.7 1.6 copy.33
  258.3 1.0 fusion.43
  259.3 1.0 fusion.44
  260.3 1.4 fusion.46
  261.8 0.9 copy-done.2
  262.7 0.6 dynamic_slice.31
  263.9 0.8 dynamic_slice.32
  264.7 0.1 broadcast_compare_fusion.2
  264.8 3.1 %constant_dynamic-slice_fusion.3 = (bf16[512,1408]{1,0:T(8,128)(2,1)S(1)}, bf16[512,1408]{1,0:T(8,128)(2,1)}) fusion(bf16[2048,1408]{1,0:T(8,128)(2,1)} %get-tuple-element.274, s32[]{:T(128)S(6)} %select_n.132, bf16[2048,1408]{1,0:T(8,128)(2,1)} %get-tuple-element.272), kind=kLoop, calls=%fused_computation.17.clone.1 | loop fusion | bytes 5767172 | tf_op jit(solution)/shard_map/while/body/eval_jaxpr/dynamic_slice | solution.py:105
  268.0 1.7 copy.32
  269.7 1.6 copy.33
  271.3 1.0 fusion.43
  272.3 1.0 fusion.44
  273.4 1.4 fusion.46
  274.8 0.9 copy-done.2
  275.7 1.2 divide_convert_fusion
  276.9 0.9 copy.26
  (47 shorter events, 0.7 us)
Async XLA Ops:
  27.4 31.1 %all-to-all-start = ((s32[16,1,16]{2,1,0:T(1,128)}), s32[16,1,16]{2,1,0:T(1,128)S(1)}, u32[]{:S(2)}, u32[]{:S(2)}) async-start(s32[16,1,16]{2,1,0:T(1,128)} %bitcast.7), calls=%async_computation | async-start | bytes 16384 | tf_op jit(solution)/shard_map/all_to_all | solution.py:79
  58.5 28.6 %all-to-all-start.1 = ((bf16[16,16,1408]{2,1,0:T(8,128)(2,1)}), bf16[16,16,1408]{2,1,0:T(8,128)(2,1)S(1)}, u32[]{:S(2)}, u32[]{:S(2)}) async-start(bf16[16,16,1408]{2,1,0:T(8,128)(2,1)} %scatter_fusion.1), calls=%async_computation.1 | async-start | bytes 1441792 | tf_op jit(solution)/shard_map/all_to_all | solution.py:78
  65.9 91.7 %all-gather.5.cloned.1.call-start = ((), (), s32[]{:S(2)}) async-start(), calls=%async_computation.3 | async-start | bytes 6127616 | tf_op jit(solution)/shard_map/all_gather | solution.py:98
  96.7 127.0 %all-gather.3.cloned.1.call-start = ((), (), s32[]{:S(2)}) async-start(), calls=%async_computation.2 | async-start | bytes 6127616 | tf_op jit(solution)/shard_map/all_gather | solution.py:97
  232.2 2.1 copy-start
  232.2 2.1 copy-start.1
  235.7 0.9 copy-start.2
  245.3 2.1 copy-start
  245.3 2.1 copy-start.1
  248.8 0.9 copy-start.2
  258.3 2.1 copy-start
  258.3 2.1 copy-start.1
  261.8 0.9 copy-start.2
  271.3 2.1 copy-start
  271.3 2.1 copy-start.1
  274.8 0.9 copy-start.2
Sparse Core Ops, SparseCore 0:
  96.8 60.7 all-gather.4
  160.0 63.6 all-gather.2
where the time goes:
time: 286 us; the launch traced here: 285 us
  waiting for transfers between devices  146 us (51%)
  local copies, waits for them, and re-layouts  80.1 us (28%)
  starting transfers between devices  17.4 us (6%)
  matrix products  16 us (6%)
  between operations  13.5 us (5%)
  other arithmetic  8.65 us (3%)
  loops' own time  2.95 us (1%)
    all_gather x1, waiting for transfers between devices, per_device(): key_piece = lax.all_gather(key_rows, 'seq', axis=0, tiled=True)  66.1 us
    all_gather x1, waiting for transfers between devices, per_device(): value_piece = lax.all_gather(value_rows, 'seq', axis=0, tiled=True)  59.2 us
    scatter x1, local copies, waits for them, and re-layouts, per_device(): outgoing = jnp.zeros((pack_count, capacity, model_width), jnp.bfloat16).a...  20.2 us
    all_to_all x1, waiting for transfers between devices, per_device(): lax.all_to_all(outgoing, 'dp', split_axis=0, concat_axis=0, tiled=True)  20 us
    dynamic_slice x8, local copies, waits for them, and re-layouts, advance(): lax.dynamic_slice_in_dim(value_piece, begin_row, block_rows, 0)  19 us
    scatter x1, local copies, waits for them, and re-layouts, per_device(): jnp.full((pack_count, capacity), count_rows, jnp.int32)  18.5 us
    all_to_all x1, starting transfers between devices, per_device(): lax.all_to_all(out_slots, 'dp', split_axis=0, concat_axis=0, tiled=True)  10 us
    all_to_all x1, starting transfers between devices, per_device(): lax.all_to_all(outgoing, 'dp', split_axis=0, concat_axis=0, tiled=True)  7.32 us
  transfers between devices with their start and end apart: 4, of which 3 were waited for; matrix products, arithmetic and copies ran while one was open for 8% of the time, Pallas kernels for 0%

commit v1 on v0

v1 whole, which is shorter than its diff:
```python
import functools
import math

import jax
import jax.numpy as jnp
from jax import lax
from jax.experimental import pallas as pl
from jax.experimental.pallas import tpu as pltpu
from jax.sharding import PartitionSpec as P

HD = 88
UNIT = 256
EPSILON = 1e-06
MASKED_SCORE = -1e30
MESH = pl.DeviceIdType.MESH
F32, BF16, I32 = jnp.float32, jnp.bfloat16, jnp.int32


def iota(shape, dim):
    return lax.broadcasted_iota(I32, shape, dim)


def dot(a, b):
    return jnp.dot(a, b, preferred_element_type=F32)


def ring_order(size):
    return sorted(range(1, size), key=lambda d: -min(d, size - d))


def kernel(
    n_dp, n_seq, tok, dest, seg, w_hbm, out,
    w, sendx, recvx, dests, y_t, sendkv, recvkv, sendq, recvq, keys, values_t, scores, sendo, recvo,
    w_sem, d_send, d_recv, x_send, x_recv, kv_send, kv_recv, q_send, q_recv, o_send, o_recv,
):
    rows, width = tok.shape[1:]
    slots = sendx.shape[0] // n_dp
    pack = n_seq * rows
    pair = UNIT // rows
    units = pack // UNIT
    n_z, n_x = n_dp // 2, math.isqrt(n_seq)
    n_y = n_seq // n_x
    dp, me = lax.axis_index("dp"), lax.axis_index("seq")
    z, core = dp // 2, dp % 2
    y_pos, x_pos = me // n_x, me % n_x

    w_copy = pltpu.make_async_copy(w_hbm, w, w_sem)
    w_copy.start()

    dp_peers = [
        (((z + dz) % n_z) * 2 + c) for c in (0, 1) for dz in ring_order(n_z)
    ] + [z * 2 + (1 - core)]
    dist = lambda d, n: min(d, n - d)
    moves = sorted(
        [(a, b) for a in range(n_y) for b in range(n_x) if (a, b) != (0, 0)],
        key=lambda m: -(dist(m[0], n_y) + dist(m[1], n_x)),
    )
    seq_peers = [((y_pos + a) % n_y) * n_x + (x_pos + b) % n_x for a, b in moves]

    barrier = pltpu.get_barrier_semaphore()
    for p in dp_peers:
        pl.semaphore_signal(barrier, inc=1, device_id=(p, me), device_id_type=MESH)
    for s in seq_peers:
        pl.semaphore_signal(barrier, inc=1, device_id=(dp, s), device_id_type=MESH)

    shift = pack.bit_length() - 1
    own_dest = dest[...]
    dests[dp] = own_dest
    widened = tok[0].astype(F32)
    center = jnp.mean(widened, axis=-1, keepdims=True)
    spread = jnp.mean(jnp.square(widened - center), axis=-1, keepdims=True)
    normed = ((widened - center) * lax.rsqrt(spread + EPSILON)).astype(BF16)
    earlier = (iota((rows, rows), 0) < iota((rows, rows), 1)).astype(F32).astype(BF16)
    own_pack = lax.shift_right_logical(own_dest, shift)
    member = (iota((n_dp, rows), 0) == own_pack).astype(F32)
    rank = jnp.sum(member * dot(member.astype(BF16), earlier), axis=0, keepdims=True)
    slot = own_pack * slots + rank.astype(I32)
    pick = (iota((n_dp * slots, rows), 0) == slot).astype(F32).astype(BF16)
    sendx[...] = dot(pick, normed).astype(BF16)

    pl.semaphore_wait(barrier, len(dp_peers) + len(seq_peers))

    def dest_copy(p, slot_of):
        return pltpu.make_async_remote_copy(
            dest, dests.at[slot_of], d_send.at[p], d_recv.at[slot_of],
            device_id=(p, me), device_id_type=MESH,
        )

    def x_copy(p, slot_of):
        return pltpu.make_async_remote_copy(
            sendx.at[pl.ds(pl.multiple_of(p * slots, slots), slots)],
            recvx.at[pl.ds(pl.multiple_of(slot_of * slots, slots), slots)],
            x_send.at[p], x_recv.at[slot_of],
            device_id=(p, me), device_id_type=MESH,
        )

    def seq_copy(src, dst, send, recv, s, slot_of):
        return pltpu.make_async_remote_copy(
            src.at[s], dst.at[slot_of], send.at[s], recv.at[slot_of],
            device_id=(dp, s), device_id_type=MESH,
        )

    for p in dp_peers:
        dest_copy(p, dp).start()
    for p in dp_peers:
        x_copy(p, dp).start()
    own = pl.ds(pl.multiple_of(dp * slots, slots), slots)
    recvx[own, :] = sendx[own, :]

    for p in dp_peers:
        dest_copy(p, p).wait_recv()
    all_dest = jnp.concatenate([dests[i] for i in range(n_dp)], axis=0)
    here = (lax.shift_right_logical(all_dest, shift) == dp).astype(F32)
    ranks = dot(here.astype(BF16), earlier).astype(I32)
    place = (all_dest & (pack - 1)) - me * rows
    pieces = []
    for i in range(n_dp):
        by_slot = jnp.where(
            iota((slots, rows), 0) == ranks[i : i + 1, :], here[i : i + 1, :], 0.0
        ).astype(BF16)
        by_place = (iota((rows, rows), 0) == place[i : i + 1, :]).astype(F32).astype(BF16)
        pieces.append(
            lax.dot_general(
                by_slot, by_place, (((1,), (1,)), ((), ())), preferred_element_type=F32
            )
        )
    unsort = jnp.concatenate(pieces, axis=0).T.astype(BF16)

    w_copy.wait()
    for p in dp_peers:
        x_copy(p, p).wait_recv()
    x = dot(unsort, recvx[...]).astype(BF16)

    def project(begin, end):
        for c0 in range(begin, end, 256):
            c1 = min(c0 + 256, end)
            y_t[c0:c1, :] = dot(x, w[:, c0:c1]).T

    def kv_of(s):
        k = y_t[pl.ds(pl.multiple_of(width + s * HD, 8), HD), :]
        v = y_t[pl.ds(pl.multiple_of(2 * width + s * HD, 8), HD), :]
        return jnp.concatenate([k, v], axis=0).astype(BF16)

    pad = jnp.zeros((8, rows), F32)

    def q_of(s):
        q = y_t[pl.ds(pl.multiple_of(s * HD, 8), HD), :]
        return jnp.concatenate([q, pad], axis=0).astype(BF16)

    project(width, 3 * width)
    for s in seq_peers:
        sendkv[s] = kv_of(s)
        seq_copy(sendkv, recvkv, kv_send, kv_recv, s, me).start()
    recvkv[me] = kv_of(me)
    project(0, width)
    for s in seq_peers:
        sendq[s] = q_of(s)
        seq_copy(sendq, recvq, q_send, q_recv, s, me).start()
    recvq[me] = q_of(me)

    def unpack(s):
        block = recvkv[s].astype(F32)
        k = jnp.concatenate([block[:HD], jnp.zeros((rows - HD, rows), F32)], axis=0)
        at = pl.ds(pl.multiple_of(s * rows, rows), rows)
        keys[at, :] = k.T.astype(BF16)
        values_t[:, at] = jnp.concatenate([block[HD:], pad], axis=0).astype(BF16)

    unpack(me)
    for s in seq_peers[::-1]:
        seq_copy(sendkv, recvkv, kv_send, kv_recv, s, s).wait_recv()
        unpack(s)

    factor = HD ** (-0.5) * math.log2(math.e)
    filler = jnp.zeros((keys.shape[1] - sendq.shape[1], UNIT), BF16)

    def attend(j):
        q = jnp.concatenate([recvq[j * pair + i] for i in range(pair)], axis=1)
        q = jnp.concatenate([q, filler], axis=0)
        q_seg = seg[:, pl.ds(pl.multiple_of(j * UNIT, UNIT), UNIT)]
        peak = jnp.full((1, UNIT), MASKED_SCORE, F32)
        same = []
        for u in range(units):
            span = slice(u * UNIT, (u + 1) * UNIT)
            part = dot(keys[span, :], q)
            scores[span, :] = part
            same.append(seg[:, span] == q_seg)
            peak = jnp.where(
                same[u], jnp.maximum(peak, jnp.max(part, axis=0, keepdims=True)), peak
            )
        totals = jnp.zeros((1, UNIT), F32)
        mixed = jnp.zeros((values_t.shape[0], UNIT), F32)
        for u in range(units):
            span = slice(u * UNIT, (u + 1) * UNIT)
            level = jnp.where(same[u], peak, -MASKED_SCORE)
            weights = jnp.exp2((scores[span, :] - level) * factor)
            totals += jnp.sum(weights, axis=0, keepdims=True)
            mixed += dot(values_t[:, span], weights.astype(BF16))
        return (mixed / totals).astype(BF16)

    own_j = me // pair

    @pl.loop(1, units)
    def _(k):
        j = (own_j + k) % units
        for i in range(pair):
            s = j * pair + i
            seq_copy(sendq, recvq, q_send, q_recv, s, s).wait_recv()
        mixed = attend(j)
        for i in range(pair):
            s = j * pair + i
            sendo[s] = mixed[:, i * rows : (i + 1) * rows]
            seq_copy(sendo, recvo, o_send, o_recv, s, me).start()

    for i in range(1, pair):
        s = own_j * pair + (me + i) % pair
        seq_copy(sendq, recvq, q_send, q_recv, s, s).wait_recv()
    mixed = attend(own_j)
    for i in range(pair):
        sendo[own_j * pair + i] = mixed[:, i * rows : (i + 1) * rows]
    recvo[me] = sendo[me]
    for i in range(1, pair):
        s = own_j * pair + (me + i) % pair
        seq_copy(sendo, recvo, o_send, o_recv, s, me).start()

    for s in seq_peers:
        seq_copy(sendo, recvo, o_send, o_recv, s, s).wait_recv()
    for h in range(n_seq):
        y_t[h * HD : (h + 1) * HD, :] = recvo[h].astype(F32)[:HD]
    for c0 in range(0, width, 128):
        c1 = min(c0 + 128, width)
        out[0, :, c0:c1] = y_t[c0:c1, :].T.astype(BF16)

    for p in dp_peers:
        dest_copy(p, dp).wait_send()
        x_copy(p, dp).wait_send()
    for s in seq_peers:
        seq_copy(sendkv, recvkv, kv_send, kv_recv, s, me).wait_send()
        seq_copy(sendq, recvq, q_send, q_recv, s, me).wait_send()
        seq_copy(sendo, recvo, o_send, o_recv, s, me).wait_send()


def per_device(n_dp, n_seq, tok, dest, seg, projection):
    rows, width = tok.shape[1:]
    slots = 2 * rows // n_dp
    pack = n_seq * rows
    dma = pltpu.SemaphoreType.DMA
    vmem = pl.BlockSpec(memory_space=pltpu.VMEM)
    return pl.pallas_call(
        functools.partial(kernel, n_dp, n_seq),
        out_shape=jax.ShapeDtypeStruct(tok.shape, BF16),
        in_specs=[vmem, vmem, vmem, pl.BlockSpec(memory_space=pl.ANY)],
        out_specs=vmem,
        scratch_shapes=[
            pltpu.VMEM(projection.shape, BF16),
            pltpu.VMEM((n_dp * slots, width), BF16),
            pltpu.VMEM((n_dp * slots, width), BF16),
            pltpu.VMEM((n_dp, 1, rows), I32),
            pltpu.VMEM((3 * width, rows), F32),
            pltpu.VMEM((n_seq, 2 * HD, rows), BF16),
            pltpu.VMEM((n_seq, 2 * HD, rows), BF16),
            pltpu.VMEM((n_seq, HD + 8, rows), BF16),
            pltpu.VMEM((n_seq, HD + 8, rows), BF16),
            pltpu.VMEM((pack, 128), BF16),
            pltpu.VMEM((HD + 8, pack), BF16),
            pltpu.VMEM((pack, UNIT), F32),
            pltpu.VMEM((n_seq, HD + 8, rows), BF16),
            pltpu.VMEM((n_seq, HD + 8, rows), BF16),
            dma,
        ]
        + [dma((n_dp,))] * 4
        + [dma((n_seq,))] * 6,
        compiler_params=pltpu.CompilerParams(
            collective_id=0, has_side_effects=True, vmem_limit_bytes=56 * 2**20
        ),
    )(tok, dest, seg, projection)


def solution(mesh):
    placed = (P("dp", "seq", None), P("dp", "seq"), P("dp", None), P())
    return jax.shard_map(
        functools.partial(per_device, mesh.shape["dp"], mesh.shape["seq"]),
        mesh=mesh,
        in_specs=placed,
        out_specs=P("dp", "seq", None),
        check_vma=False,
    )
```

time: 286 us -> 55.8 us (0.20)
  waiting for transfers between devices: 146 us -> 0 us
  local copies, waits for them, and re-layouts: 80.1 us -> 1.75 us
  Pallas kernels: 0 us -> 53.9 us
  starting transfers between devices: 17.4 us -> 0 us
  matrix products: 16 us -> 0 us
  between operations: 13.5 us -> 0.01 us
  other arithmetic: 8.65 us -> 0 us
  loops' own time: 2.95 us -> 0 us
    all_gather x2 -> x0, waiting for transfers between devices: 125 us -> none  [the longest x1 66.1 us: per_device(): key_piece = lax.all_gather(key_rows, 'seq', axis=0, tiled=True)]
    pallas_call x0 -> x1, Pallas kernels: none -> 53.9 us  [per_device(): pl.pallas_call(functools.partial(kernel, n_dp, n_seq), out_shape=jax.Shap...]
    scatter x3 -> x0, local copies, waits for them, and re-layouts: 40.4 us -> none  [the longest x1 20.2 us: per_device(): outgoing = jnp.zeros((pack_count, capacity, model_width), jnp.bfloat16).a...]
    dynamic_slice x21 -> x0, local copies, waits for them, and re-layouts: 31.8 us -> none  [the longest x8 19 us: advance(): lax.dynamic_slice_in_dim(value_piece, begin_row, block_rows, 0)]
    all_to_all x2 -> x0, waiting for transfers between devices: 20 us -> none  [the longest x1 20 us: per_device(): lax.all_to_all(outgoing, 'dp', split_axis=0, concat_axis=0, tiled=True)]
    all_to_all x2 -> x0, starting transfers between devices: 17.3 us -> none  [the longest x1 10 us: per_device(): lax.all_to_all(out_slots, 'dp', split_axis=0, concat_axis=0, tiled=True)]
    dot_general x9 -> x0, matrix products: 16 us -> none  [the longest x1 6.36 us: per_device(): jnp.dot(normalize(packed), projection, preferred_element_type=jnp.float32)]
    reduce_sum x7 -> x0, other arithmetic: 4.57 us -> none  [the longest x4 4.02 us: update(): totals = totals * factor + jnp.sum(weights, axis=-1)]
  transfers between devices with their start and end apart: 4 -> 0, of which waited for: 3 -> 0; matrix products, arithmetic and copies ran while one was open for 8% -> 0% of each run, Pallas kernels for 0% -> 0%
where the time goes in v1:
time: 55.8 us; the launch traced here: 55.7 us
  Pallas kernels  53.9 us (97%)
  local copies, waits for them, and re-layouts  1.75 us (3%)
    pallas_call x1, Pallas kernels, per_device(): pl.pallas_call(functools.partial(kernel, n_dp, n_seq), out_shape=jax.Shap...  53.9 us
    unnamed x1, local copies, waits for them, and re-layouts  1.75 us

profile of v1, /device:TPU:1, one launch (start us, length us, event | category | flops | bytes accessed | tf_op | source)
XLA Modules:
  0.0 55.7 jit_solution(1680943151116141173)
XLA Ops:
  0.0 53.9 %shard_map.46 = bf16[1,128,1408]{2,1,0:T(8,128)(2,1)} custom-call(bf16[1,128,1408]{2,1,0:T(8,128)(2,1)} %tok.1, s32[1,128]{1,0:T(1,128)} %dest.1, s32[1,2048]{1,0:T(1,128)} %seg.1, bf16[1408,4224]{1,0:T(8,128)(2,1)} %w_hbm.1), custom_call_target="tpu_custom_call" | custom-call | tf_op jit(solution)/shard_map/pallas_call | solution.py:248
  53.9 1.7 %copy.6 = bf16[1,128,1408]{2,1,0:T(8,128)(2,1)} copy(bf16[1,128,1408]{2,1,0:T(8,128)(2,1)} %shard_map.46) | data formatting | bytes 720896

commit v2 on v1

v2 whole, which is shorter than its diff:
```python
import functools
import math

import jax
import jax.numpy as jnp
from jax import lax
from jax.experimental import pallas as pl
from jax.experimental.pallas import tpu as pltpu
from jax.sharding import PartitionSpec as P

HD = 88
UNIT = 256
EPSILON = 1e-06
MASKED_SCORE = -1e30
MESH = pl.DeviceIdType.MESH
F32, BF16, I32 = jnp.float32, jnp.bfloat16, jnp.int32


def iota(shape, dim):
    return lax.broadcasted_iota(I32, shape, dim)


def dot(a, b):
    return jnp.dot(a, b, preferred_element_type=F32)


def ring_order(size):
    return sorted(range(1, size), key=lambda d: -min(d, size - d))


def kernel(
    n_dp, n_seq, tok_hbm, dest_hbm, seg_hbm, w_hbm, heads_out,
    tok, seg, w, sendx, recvx, dests, y_t, sendkv, recvkv, sendq, recvq, keys, values_t, scores_a, scores_b, sendo,
    in_sem, d_send, d_recv, x_send, x_recv, kv_send, kv_recv, q_send, q_recv, o_send, o_recv,
):
    rows, width = tok.shape
    slots = sendx.shape[0] // n_dp
    pack = n_seq * rows
    pair = UNIT // rows
    units = pack // UNIT
    n_z, n_x = n_dp // 2, math.isqrt(n_seq)
    n_y = n_seq // n_x
    dp, me = lax.axis_index("dp"), lax.axis_index("seq")
    z, core = dp // 2, dp % 2
    y_pos, x_pos = me // n_x, me % n_x

    tok_copy = pltpu.make_async_copy(tok_hbm.at[0], tok, in_sem.at[0])
    dest_copy_in = pltpu.make_async_copy(dest_hbm, dests.at[dp], in_sem.at[1])
    seg_copy = pltpu.make_async_copy(seg_hbm, seg, in_sem.at[2])
    w_copy = pltpu.make_async_copy(w_hbm, w, in_sem.at[3])
    tok_copy.start()
    dest_copy_in.start()

    dp_peers = [
        (((z + dz) % n_z) * 2 + c) for c in (0, 1) for dz in ring_order(n_z)
    ] + [z * 2 + (1 - core)]
    dist = lambda d, n: min(d, n - d)
    moves = sorted(
        [(a, b) for a in range(n_y) for b in range(n_x) if (a, b) != (0, 0)],
        key=lambda m: -(dist(m[0], n_y) + dist(m[1], n_x)),
    )
    seq_peers = [((y_pos + a) % n_y) * n_x + (x_pos + b) % n_x for a, b in moves]

    barrier = pltpu.get_barrier_semaphore()
    for p in dp_peers:
        pl.semaphore_signal(barrier, inc=1, device_id=(p, me), device_id_type=MESH)
    for s in seq_peers:
        pl.semaphore_signal(barrier, inc=1, device_id=(dp, s), device_id_type=MESH)

    seg_copy.start()
    w_copy.start()

    shift = pack.bit_length() - 1
    dest_copy_in.wait()
    own_dest = dests[dp]
    tok_copy.wait()
    widened = tok[...].astype(F32)
    center = jnp.mean(widened, axis=-1, keepdims=True)
    spread = jnp.mean(jnp.square(widened - center), axis=-1, keepdims=True)
    normed = ((widened - center) * lax.rsqrt(spread + EPSILON)).astype(BF16)
    earlier = (iota((rows, rows), 0) < iota((rows, rows), 1)).astype(F32).astype(BF16)
    own_pack = lax.shift_right_logical(own_dest, shift)
    member = (iota((n_dp, rows), 0) == own_pack).astype(F32)
    rank = jnp.sum(member * dot(member.astype(BF16), earlier), axis=0, keepdims=True)
    slot = own_pack * slots + rank.astype(I32)
    pick = (iota((n_dp * slots, rows), 0) == slot).astype(F32).astype(BF16)
    sendx[...] = dot(pick, normed).astype(BF16)

    pl.semaphore_wait(barrier, len(dp_peers) + len(seq_peers))

    def dest_copy(p, slot_of):
        return pltpu.make_async_remote_copy(
            dests.at[dp], dests.at[slot_of], d_send, d_recv,
            device_id=(p, me), device_id_type=MESH,
        )

    def x_copy(p, slot_of):
        return pltpu.make_async_remote_copy(
            sendx.at[pl.ds(pl.multiple_of(p * slots, slots), slots)],
            recvx.at[pl.ds(pl.multiple_of(slot_of * slots, slots), slots)],
            x_send, x_recv,
            device_id=(p, me), device_id_type=MESH,
        )

    def seq_copy(src, dst, send, recv, s, slot_of):
        return pltpu.make_async_remote_copy(
            src.at[s], dst.at[slot_of], send, recv,
            device_id=(dp, s), device_id_type=MESH,
        )

    def wait_bytes(ref, count, sem):
        pltpu.make_async_copy(ref.at[pl.ds(0, count)], ref.at[pl.ds(0, count)], sem).wait()

    for p in dp_peers[:2]:
        x_copy(p, dp).start()
    for p in dp_peers[:2]:
        dest_copy(p, dp).start()
    for p in dp_peers[2:]:
        x_copy(p, dp).start()
        dest_copy(p, dp).start()
    own = pl.ds(pl.multiple_of(dp * slots, slots), slots)
    recvx[own, :] = sendx[own, :]

    wait_bytes(dests, n_dp - 1, d_recv)
    all_dest = jnp.concatenate([dests[i] for i in range(n_dp)], axis=0)
    here = (lax.shift_right_logical(all_dest, shift) == dp).astype(F32)
    ranks = dot(here.astype(BF16), earlier).astype(I32)
    place = (all_dest & (pack - 1)) - me * rows
    pieces = []
    for i in range(n_dp):
        by_slot = jnp.where(
            iota((slots, rows), 0) == ranks[i : i + 1, :], here[i : i + 1, :], 0.0
        ).astype(BF16)
        by_place = (iota((rows, rows), 0) == place[i : i + 1, :]).astype(F32).astype(BF16)
        pieces.append(
            lax.dot_general(
                by_slot, by_place, (((1,), (1,)), ((), ())), preferred_element_type=F32
            )
        )
    unsort = jnp.concatenate(pieces, axis=0).T.astype(BF16)

    w_copy.wait()
    wait_bytes(recvx, (n_dp - 1) * slots, x_recv)
    x = dot(unsort, recvx[...]).astype(BF16)

    def project(begin, end):
        for c0 in range(begin, end, 256):
            c1 = min(c0 + 256, end)
            y_t[c0:c1, :] = dot(x, w[:, c0:c1]).T

    def kv_of(s):
        k = y_t[pl.ds(pl.multiple_of(width + s * HD, 8), HD), :]
        v = y_t[pl.ds(pl.multiple_of(2 * width + s * HD, 8), HD), :]
        return jnp.concatenate([k, v], axis=0).astype(BF16)

    pad = jnp.zeros((8, rows), F32)

    def q_of(s):
        q = y_t[pl.ds(pl.multiple_of(s * HD, 8), HD), :]
        return jnp.concatenate([q, pad], axis=0).astype(BF16)

    project(width, 3 * width)
    for s in seq_peers:
        sendkv[s] = kv_of(s)
        seq_copy(sendkv, recvkv, kv_send, kv_recv.at[me], s, me).start()
    recvkv[me] = kv_of(me)
    project(0, width)
    for s in seq_peers:
        sendq[s] = q_of(s)
        seq_copy(sendq, recvq, q_send, q_recv.at[me // pair], s, me).start()
    recvq[me] = q_of(me)

    def unpack(s):
        block = recvkv[s].astype(F32)
        k = jnp.concatenate([block[:HD], jnp.zeros((rows - HD, rows), F32)], axis=0)
        at = pl.ds(pl.multiple_of(s * rows, rows), rows)
        keys[at, :] = k.T.astype(BF16)
        values_t[:, at] = jnp.concatenate([block[HD:], pad], axis=0).astype(BF16)

    unpack(me)
    seg_copy.wait()
    for s in seq_peers:
        seq_copy(sendkv, recvkv, kv_send, kv_recv.at[s], s, s).wait_recv()
        unpack(s)

    factor = HD ** (-0.5) * math.log2(math.e)
    filler = jnp.zeros((keys.shape[1] - sendq.shape[1], UNIT), BF16)
    chunk = min(4, units)

    def spans(g):
        return slice(g * chunk * UNIT, (g + 1) * chunk * UNIT)

    def load(j, count):
        wait_bytes(recvq, count, q_recv.at[j])
        q = jnp.concatenate([recvq[j * pair + i] for i in range(pair)], axis=1)
        q_seg = seg[:, pl.ds(pl.multiple_of(j * UNIT, UNIT), UNIT)]
        same = [seg[:, u * UNIT : (u + 1) * UNIT] == q_seg for u in range(units)]
        return jnp.concatenate([q, filler], axis=0), same

    def score(g, q, same, peak, held):
        part = dot(keys[spans(g), :], q)
        held[spans(g), :] = part
        for i in range(chunk):
            top = jnp.max(part[i * UNIT : (i + 1) * UNIT], axis=0, keepdims=True)
            peak = jnp.where(same[g * chunk + i], jnp.maximum(peak, top), peak)
        return peak

    def mix(g, same, peak, held, totals, mixed):
        pieces = []
        for u in range(g * chunk, (g + 1) * chunk):
            level = jnp.where(same[u], peak, -MASKED_SCORE)
            piece = jnp.exp2((held[u * UNIT : (u + 1) * UNIT, :] - level) * factor)
            totals = totals + jnp.sum(piece.reshape(UNIT // 8, 8, UNIT), axis=0)
            pieces.append(piece.astype(BF16))
        weights = jnp.concatenate(pieces, axis=0)
        return totals, mixed + dot(values_t[:, spans(g)], weights)

    own_j = me // pair
    order = [(own_j + 1 + k) % units for k in range(units)]
    held = (scores_a, scores_b)
    floor = jnp.full((1, UNIT), MASKED_SCORE, F32)
    q, same = load(order[0], pair)
    peak = floor
    for g in range(units // chunk):
        peak = score(g, q, same, peak, held[0])
    for k in range(units):
        now_same, now_peak = same, peak
        last = k == units - 1
        if not last:
            q, same = load(order[k + 1], pair - 1 if k + 1 == units - 1 else pair)
            peak = floor
        totals = jnp.zeros((8, UNIT), F32)
        mixed = jnp.zeros((values_t.shape[0], UNIT), F32)
        for g in range(units // chunk):
            if not last:
                peak = score(g, q, same, peak, held[(k + 1) % 2])
            totals, mixed = mix(g, now_same, now_peak, held[k % 2], totals, mixed)
        result = (mixed / jnp.sum(totals, axis=0, keepdims=True)).astype(BF16)
        for i in range(pair):
            sendo[order[k] * pair + i] = result[:, i * rows : (i + 1) * rows]
        for i in range(1 if last else 0, pair):
            s = own_j * pair + (me + i) % pair if last else order[k] * pair + i
            seq_copy(sendo, heads_out, o_send, o_recv, s, me).start()
    own_copy = pltpu.make_async_copy(sendo.at[me], heads_out.at[me], in_sem.at[4])
    own_copy.start()

    wait_bytes(dests, n_dp - 1, d_send)
    wait_bytes(sendx, (n_dp - 1) * slots, x_send)
    wait_bytes(sendkv, n_seq - 1, kv_send)
    wait_bytes(sendq, n_seq - 1, q_send)
    own_copy.wait()
    wait_bytes(sendo, n_seq - 1, o_send)
    wait_bytes(heads_out, n_seq - 1, o_recv)


def assemble(heads, out, stacked):
    for h in range(heads.shape[0]):
        stacked[h * HD : (h + 1) * HD, :] = heads[h].astype(F32)[:HD]
    width = out.shape[2]
    for c0 in range(0, width, 128):
        c1 = min(c0 + 128, width)
        out[0, :, c0:c1] = stacked[c0:c1, :].T.astype(BF16)


def per_device(n_dp, n_seq, tok, dest, seg, projection):
    rows, width = tok.shape[1:]
    slots = 2 * rows // n_dp
    pack = n_seq * rows
    dma = pltpu.SemaphoreType.DMA
    vmem = pl.BlockSpec(memory_space=pltpu.VMEM)
    anywhere = pl.BlockSpec(memory_space=pl.ANY)
    heads = pl.pallas_call(
        functools.partial(kernel, n_dp, n_seq),
        out_shape=jax.ShapeDtypeStruct((n_seq, HD + 8, rows), BF16),
        in_specs=[anywhere] * 4,
        out_specs=anywhere,
        scratch_shapes=[
            pltpu.VMEM((rows, width), BF16),
            pltpu.VMEM(seg.shape, I32),
            pltpu.VMEM(projection.shape, BF16),
            pltpu.VMEM((n_dp * slots, width), BF16),
            pltpu.VMEM((n_dp * slots, width), BF16),
            pltpu.VMEM((n_dp, 1, rows), I32),
            pltpu.VMEM((3 * width, rows), F32),
            pltpu.VMEM((n_seq, 2 * HD, rows), BF16),
            pltpu.VMEM((n_seq, 2 * HD, rows), BF16),
            pltpu.VMEM((n_seq, HD + 8, rows), BF16),
            pltpu.VMEM((n_seq, HD + 8, rows), BF16),
            pltpu.VMEM((pack, 128), BF16),
            pltpu.VMEM((HD + 8, pack), BF16),
            pltpu.VMEM((pack, UNIT), F32),
            pltpu.VMEM((pack, UNIT), F32),
            pltpu.VMEM((n_seq, HD + 8, rows), BF16),
            dma((5,)),
            dma,
            dma,
            dma,
            dma,
            dma,
            dma((n_seq,)),
            dma,
            dma((pack // UNIT,)),
            dma,
            dma,
        ],
        compiler_params=pltpu.CompilerParams(
            collective_id=0, has_side_effects=True, vmem_limit_bytes=56 * 2**20
        ),
    )(tok, dest, seg, projection)
    return pl.pallas_call(
        assemble,
        out_shape=jax.ShapeDtypeStruct(tok.shape, BF16),
        in_specs=[vmem],
        out_specs=vmem,
        scratch_shapes=[pltpu.VMEM((width, rows), F32)],
        compiler_params=pltpu.CompilerParams(vmem_limit_bytes=32 * 2**20),
    )(heads)


def solution(mesh):
    placed = (P("dp", "seq", None), P("dp", "seq"), P("dp", None), P())
    return jax.shard_map(
        functools.partial(per_device, mesh.shape["dp"], mesh.shape["seq"]),
        mesh=mesh,
        in_specs=placed,
        out_specs=P("dp", "seq", None),
        check_vma=False,
    )
```

time: 55.8 us -> 52 us (0.932)
  Pallas kernels: 53.9 us -> 50.9 us
  local copies, waits for them, and re-layouts: 1.75 us -> 0.99 us
    pallas_call x1, Pallas kernels: 53.9 us -> 50 us  [per_device(): pl.pallas_call(functools.partial(kernel, n_dp, n_seq), out_shape=jax.Shap...]
    pallas_call x0 -> x1, Pallas kernels: none -> 0.91 us  [per_device(): pl.pallas_call(assemble, out_shape=jax.ShapeDtypeStruct(tok.shape, BF16),...]
    unnamed x1 -> x2, local copies, waits for them, and re-layouts: 1.75 us -> 0.99 us
where the time goes in v2:
time: 52 us; the launch traced here: 51.9 us
  Pallas kernels  50.9 us (98%)
  local copies, waits for them, and re-layouts  0.99 us (2%)
    pallas_call x1, Pallas kernels, per_device(): pl.pallas_call(functools.partial(kernel, n_dp, n_seq), out_shape=jax.Shap...  50 us

profile of v2, /device:TPU:1, one launch (start us, length us, event | category | flops | bytes accessed | tf_op | source)
XLA Modules:
  0.0 51.9 jit_solution(16214664227081158219)
XLA Ops:
  0.0 50.0 %shard_map.46.heads = bf16[16,96,128]{2,1,0:T(8,128)(2,1)} custom-call(bf16[1,128,1408]{2,1,0:T(8,128)(2,1)} %tok_hbm.1, s32[1,128]{1,0:T(1,128)} %dest_hbm.1, s32[1,2048]{1,0:T(1,128)} %seg_hbm.1, bf16[1408,4224]{1,0:T(8,128)(2,1)} %w_hbm.1), custom_call_target="tpu_custom_call" | custom-call | tf_op jit(solution)/shard_map/pallas_call | solution.py:272
  50.0 0.0 copy-start
  50.0 1.0 %copy-done = bf16[16,96,128]{2,1,0:T(8,128)(2,1)S(1)} copy-done((bf16[16,96,128]{2,1,0:T(8,128)(2,1)S(1)}, bf16[16,96,128]{2,1,0:T(8,128)(2,1)}, u32[]{:S(2)}) %copy-start) | copy-done | bytes 393240
  51.0 0.9 %shard_map.47 = bf16[1,128,1408]{2,1,0:T(8,128)(2,1)} custom-call(bf16[16,96,128]{2,1,0:T(8,128)(2,1)S(1)} %copy-done), custom_call_target="tpu_custom_call" | custom-call | tf_op jit(solution)/shard_map/pallas_call | solution.py:310
Async XLA Ops:
  50.0 1.0 %copy-start = (bf16[16,96,128]{2,1,0:T(8,128)(2,1)S(1)}, bf16[16,96,128]{2,1,0:T(8,128)(2,1)}, u32[]{:S(2)}) copy-start(bf16[16,96,128]{2,1,0:T(8,128)(2,1)} %shard_map.46.heads) | copy-start | bytes 1179652

commit v3 on v2

--- a/solution.py
+++ b/solution.py
@@ -159,16 +159,16 @@
         q = y_t[pl.ds(pl.multiple_of(s * HD, 8), HD), :]
         return jnp.concatenate([q, pad], axis=0).astype(BF16)
 
+    project(0, width)
+    for s in seq_peers:
+        sendq[s] = q_of(s)
+        seq_copy(sendq, recvq, q_send, q_recv.at[me // pair], s, me).start()
+    recvq[me] = q_of(me)
     project(width, 3 * width)
     for s in seq_peers:
         sendkv[s] = kv_of(s)
         seq_copy(sendkv, recvkv, kv_send, kv_recv.at[me], s, me).start()
     recvkv[me] = kv_of(me)
-    project(0, width)
-    for s in seq_peers:
-        sendq[s] = q_of(s)
-        seq_copy(sendq, recvq, q_send, q_recv.at[me // pair], s, me).start()
-    recvq[me] = q_of(me)
 
     def unpack(s):
         block = recvkv[s].astype(F32)

time: 52 us -> 51.2 us (0.985)
  Pallas kernels: 50.9 us -> 50.1 us
    pallas_call x1, Pallas kernels: 50 us -> 49.2 us  [per_device(): pl.pallas_call(functools.partial(kernel, n_dp, n_seq), out_shape=jax.Shap...]
where the time goes in v3:
time: 51.2 us; the launch traced here: 51.1 us
  Pallas kernels  50.1 us (98%)
  local copies, waits for them, and re-layouts  0.99 us (2%)
    pallas_call x1, Pallas kernels, per_device(): pl.pallas_call(functools.partial(kernel, n_dp, n_seq), out_shape=jax.Shap...  49.2 us

profile of v3, /device:TPU:1, one launch (start us, length us, event | category | flops | bytes accessed | tf_op | source)
XLA Modules:
  0.0 51.1 jit_solution(18061418144905635320)
XLA Ops:
  0.0 49.2 %shard_map.46.heads = bf16[16,96,128]{2,1,0:T(8,128)(2,1)} custom-call(bf16[1,128,1408]{2,1,0:T(8,128)(2,1)} %tok_hbm.1, s32[1,128]{1,0:T(1,128)} %dest_hbm.1, s32[1,2048]{1,0:T(1,128)} %seg_hbm.1, bf16[1408,4224]{1,0:T(8,128)(2,1)} %w_hbm.1), custom_call_target="tpu_custom_call" | custom-call | tf_op jit(solution)/shard_map/pallas_call | solution.py:272
  49.2 0.0 copy-start
  49.2 1.0 %copy-done = bf16[16,96,128]{2,1,0:T(8,128)(2,1)S(1)} copy-done((bf16[16,96,128]{2,1,0:T(8,128)(2,1)S(1)}, bf16[16,96,128]{2,1,0:T(8,128)(2,1)}, u32[]{:S(2)}) %copy-start) | copy-done | bytes 393240
  50.2 0.9 %shard_map.47 = bf16[1,128,1408]{2,1,0:T(8,128)(2,1)} custom-call(bf16[16,96,128]{2,1,0:T(8,128)(2,1)S(1)} %copy-done), custom_call_target="tpu_custom_call" | custom-call | tf_op jit(solution)/shard_map/pallas_call | solution.py:310
Async XLA Ops:
  49.2 1.0 %copy-start = (bf16[16,96,128]{2,1,0:T(8,128)(2,1)S(1)}, bf16[16,96,128]{2,1,0:T(8,128)(2,1)}, u32[]{:S(2)}) copy-start(bf16[16,96,128]{2,1,0:T(8,128)(2,1)} %shard_map.46.heads) | copy-start | bytes 1179652

commit v4 on v3

--- a/solution.py
+++ b/solution.py
@@ -51,9 +51,9 @@
     tok_copy.start()
     dest_copy_in.start()
 
-    dp_peers = [
+    dp_peers = [z * 2 + (1 - core)] + [
         (((z + dz) % n_z) * 2 + c) for c in (0, 1) for dz in ring_order(n_z)
-    ] + [z * 2 + (1 - core)]
+    ]
     dist = lambda d, n: min(d, n - d)
     moves = sorted(
         [(a, b) for a in range(n_y) for b in range(n_x) if (a, b) != (0, 0)],
@@ -94,11 +94,11 @@
             device_id=(p, me), device_id_type=MESH,
         )
 
-    def x_copy(p, slot_of):
+    def x_copy(p, slot_of, group):
         return pltpu.make_async_remote_copy(
             sendx.at[pl.ds(pl.multiple_of(p * slots, slots), slots)],
             recvx.at[pl.ds(pl.multiple_of(slot_of * slots, slots), slots)],
-            x_send, x_recv,
+            x_send.at[group], x_recv,
             device_id=(p, me), device_id_type=MESH,
         )
 
@@ -111,13 +111,18 @@
     def wait_bytes(ref, count, sem):
         pltpu.make_async_copy(ref.at[pl.ds(0, count)], ref.at[pl.ds(0, count)], sem).wait()
 
-    for p in dp_peers[:2]:
-        x_copy(p, dp).start()
-    for p in dp_peers[:2]:
+    for p in dp_peers[0:4]:
+        x_copy(p, dp, 0).start()
+    for p in dp_peers:
         dest_copy(p, dp).start()
-    for p in dp_peers[2:]:
-        x_copy(p, dp).start()
-        dest_copy(p, dp).start()
+    for p in dp_peers[4:8]:
+        x_copy(p, dp, 1).start()
+    wait_bytes(sendx, 4 * slots, x_send.at[0])
+    for p in dp_peers[8:12]:
+        x_copy(p, dp, 2).start()
+    wait_bytes(sendx, 4 * slots, x_send.at[1])
+    for p in dp_peers[12:15]:
+        x_copy(p, dp, 3).start()
     own = pl.ds(pl.multiple_of(dp * slots, slots), slots)
     recvx[own, :] = sendx[own, :]
 
@@ -185,7 +190,7 @@
 
     factor = HD ** (-0.5) * math.log2(math.e)
     filler = jnp.zeros((keys.shape[1] - sendq.shape[1], UNIT), BF16)
-    chunk = min(4, units)
+    chunk = min(8, units)
 
     def spans(g):
         return slice(g * chunk * UNIT, (g + 1) * chunk * UNIT)
@@ -245,7 +250,8 @@
     own_copy.start()
 
     wait_bytes(dests, n_dp - 1, d_send)
-    wait_bytes(sendx, (n_dp - 1) * slots, x_send)
+    wait_bytes(sendx, 4 * slots, x_send.at[2])
+    wait_bytes(sendx, 3 * slots, x_send.at[3])
     wait_bytes(sendkv, n_seq - 1, kv_send)
     wait_bytes(sendq, n_seq - 1, q_send)
     own_copy.wait()
@@ -294,7 +300,7 @@
             dma((5,)),
             dma,
             dma,
-            dma,
+            dma((4,)),
             dma,
             dma,
             dma((n_seq,)),

time: 51.2 us -> 50.5 us (0.986)
  Pallas kernels: 50.1 us -> 49.4 us
    pallas_call x1, Pallas kernels: 49.2 us -> 48.5 us  [per_device(): pl.pallas_call(functools.partial(kernel, n_dp, n_seq), out_shape=jax.Shap...]
where the time goes in v4:
time: 50.5 us; the launch traced here: 50.4 us
  Pallas kernels  49.4 us (98%)
  local copies, waits for them, and re-layouts  0.99 us (2%)
    pallas_call x1, Pallas kernels, per_device(): pl.pallas_call(functools.partial(kernel, n_dp, n_seq), out_shape=jax.Shap...  48.5 us

profile of v4, /device:TPU:1, one launch (start us, length us, event | category | flops | bytes accessed | tf_op | source)
XLA Modules:
  0.0 50.4 jit_solution(10938548357880041946)
XLA Ops:
  0.0 48.5 %shard_map.46.heads = bf16[16,96,128]{2,1,0:T(8,128)(2,1)} custom-call(bf16[1,128,1408]{2,1,0:T(8,128)(2,1)} %tok_hbm.1, s32[1,128]{1,0:T(1,128)} %dest_hbm.1, s32[1,2048]{1,0:T(1,128)} %seg_hbm.1, bf16[1408,4224]{1,0:T(8,128)(2,1)} %w_hbm.1), custom_call_target="tpu_custom_call" | custom-call | tf_op jit(solution)/shard_map/pallas_call | solution.py:278
  48.5 0.0 copy-start
  48.5 1.0 %copy-done = bf16[16,96,128]{2,1,0:T(8,128)(2,1)S(1)} copy-done((bf16[16,96,128]{2,1,0:T(8,128)(2,1)S(1)}, bf16[16,96,128]{2,1,0:T(8,128)(2,1)}, u32[]{:S(2)}) %copy-start) | copy-done | bytes 393240
  49.5 0.9 %shard_map.47 = bf16[1,128,1408]{2,1,0:T(8,128)(2,1)} custom-call(bf16[16,96,128]{2,1,0:T(8,128)(2,1)S(1)} %copy-done), custom_call_target="tpu_custom_call" | custom-call | tf_op jit(solution)/shard_map/pallas_call | solution.py:316
Async XLA Ops:
  48.5 1.0 %copy-start = (bf16[16,96,128]{2,1,0:T(8,128)(2,1)S(1)}, bf16[16,96,128]{2,1,0:T(8,128)(2,1)}, u32[]{:S(2)}) copy-start(bf16[16,96,128]{2,1,0:T(8,128)(2,1)} %shard_map.46.heads) | copy-start | bytes 1179652

commit v5 on v4

--- a/solution.py
+++ b/solution.py
@@ -113,10 +113,10 @@
 
     for p in dp_peers[0:4]:
         x_copy(p, dp, 0).start()
+    for p in dp_peers[4:8]:
+        x_copy(p, dp, 1).start()
     for p in dp_peers:
         dest_copy(p, dp).start()
-    for p in dp_peers[4:8]:
-        x_copy(p, dp, 1).start()
     wait_bytes(sendx, 4 * slots, x_send.at[0])
     for p in dp_peers[8:12]:
         x_copy(p, dp, 2).start()

time: 50.5 us -> 52.6 us (1.042)
  Pallas kernels: 49.4 us -> 51.5 us
    pallas_call x1, Pallas kernels: 48.5 us -> 50.6 us  [per_device(): pl.pallas_call(functools.partial(kernel, n_dp, n_seq), out_shape=jax.Shap...]
where the time goes in v5:
time: 52.6 us; the launch traced here: 52.5 us
  Pallas kernels  51.5 us (98%)
  local copies, waits for them, and re-layouts  0.99 us (2%)
    pallas_call x1, Pallas kernels, per_device(): pl.pallas_call(functools.partial(kernel, n_dp, n_seq), out_shape=jax.Shap...  50.6 us

profile of v5, /device:TPU:1, one launch (start us, length us, event | category | flops | bytes accessed | tf_op | source)
XLA Modules:
  0.0 52.5 jit_solution(9582312082652726639)
XLA Ops:
  0.0 50.6 %shard_map.46.heads = bf16[16,96,128]{2,1,0:T(8,128)(2,1)} custom-call(bf16[1,128,1408]{2,1,0:T(8,128)(2,1)} %tok_hbm.1, s32[1,128]{1,0:T(1,128)} %dest_hbm.1, s32[1,2048]{1,0:T(1,128)} %seg_hbm.1, bf16[1408,4224]{1,0:T(8,128)(2,1)} %w_hbm.1), custom_call_target="tpu_custom_call" | custom-call | tf_op jit(solution)/shard_map/pallas_call | solution.py:278
  50.6 0.0 copy-start
  50.6 1.0 %copy-done = bf16[16,96,128]{2,1,0:T(8,128)(2,1)S(1)} copy-done((bf16[16,96,128]{2,1,0:T(8,128)(2,1)S(1)}, bf16[16,96,128]{2,1,0:T(8,128)(2,1)}, u32[]{:S(2)}) %copy-start) | copy-done | bytes 393240
  51.6 0.9 %shard_map.47 = bf16[1,128,1408]{2,1,0:T(8,128)(2,1)} custom-call(bf16[16,96,128]{2,1,0:T(8,128)(2,1)S(1)} %copy-done), custom_call_target="tpu_custom_call" | custom-call | tf_op jit(solution)/shard_map/pallas_call | solution.py:316
Async XLA Ops:
  50.6 1.0 %copy-start = (bf16[16,96,128]{2,1,0:T(8,128)(2,1)S(1)}, bf16[16,96,128]{2,1,0:T(8,128)(2,1)}, u32[]{:S(2)}) copy-start(bf16[16,96,128]{2,1,0:T(8,128)(2,1)} %shard_map.46.heads) | copy-start | bytes 1179652
